TPU v7x, 128 devices: a whole 4x4x4 slice. The times are simulated.
128 devices in a mesh: frame: 8 (over z, y_hi), token: 8 (over x, y_lo), batch: 2 (over core).
Axes of the slice: x: 4, y: 4 (y_hi: 2, y_lo: 2; y = y_hi * 2 + y_lo), z: 4, core: 2. Of those that a mesh axis runs over, the one named last changes fastest.
Arguments:
- encoder_out: bfloat16 [2, 512, 512], P('batch', 'frame', 'token'), may hold values from -6 to 6
- predictor_out: bfloat16 [2, 512, 512], P('batch', 'token', 'frame'), may hold values from -6 to 6
- enc_weight: bfloat16 [512, 512], replicated, may hold values from -0.25 to 0.25
- pred_weight: bfloat16 [512, 512], replicated, may hold values from -0.25 to 0.25
- joint_bias: float32 [512], replicated, may hold values from -0.5 to 0.5
- out_weight: bfloat16 [512, 1024], replicated, may hold values from -0.076171875 to 0.076171875
- blank_occupancy: float32 [2, 512, 512], P('batch', 'frame', 'token'), may hold values from 0.05 to 1
- label_occupancy: float32 [2, 512, 512], P('batch', 'frame', 'token'), may hold values from 0.05 to 1
- frame_lengths: int32 [2], replicated, may hold values from 64 to 512, as said below
- token_lengths: int32 [2], replicated, may hold values from 64 to 511, as said below
- target_ids: int32 [2, 512], P(None, 'token'), may hold values from 1 to 1023
Outputs:
- enc_grad: float32 [2, 512, 512], P('batch', 'frame', 'token')
- pred_grad: float32 [2, 512, 512], P('batch', 'token', 'frame')
- enc_weight_grad: float32 [512, 512], P(('frame', 'token', 'batch'))
- pred_weight_grad: float32 [512, 512], P(('frame', 'token', 'batch'))
- out_weight_grad: float32 [512, 1024], P(('frame', 'token', 'batch'))
- bias_grad: float32 [512], P(('frame', 'token', 'batch'))
Inputs may be any that keep to these rules, and one draw needn't show every extreme that they name: `frame_lengths`: frames of each utterance; in every draw some utterance has all 512. `token_lengths`: target tokens of each utterance; in every draw some utterance has 511. `target_ids`: entry 0 is the blank and is never a target.
All inputs are finite; a program needn't handle non-finite values.
Results may differ from a plain program's by a relative error of at most 0.00059.
Values may be sent and summed in bfloat16 or wider, within the bound.
No kernel may reach another device: no remote copies, remote signals or barrier semaphores. Data moves between devices by JAX's collectives and lax.ppermute only.
A program may use at most 64 MiB of HBM per device.

v0:
```python
import jax
import jax.numpy as jnp
from jax import lax
from jax.sharding import PartitionSpec as P

FB = 8


def cell_hidden(frame_rows, pred_rows, joint_bias):
    inner = frame_rows[:, None, :] + pred_rows[None, :, :] + joint_bias
    return jnp.tanh(inner).astype(jnp.bfloat16).reshape(-1, inner.shape[2])


def cell_weights(blanks, labels, first_frame, first_token, frame_len, token_len):
    frame_pos = first_frame + jnp.arange(blanks.shape[0], dtype=jnp.int32)
    token_pos = first_token + jnp.arange(blanks.shape[1], dtype=jnp.int32)
    active_frame = (frame_pos < frame_len)[:, None]
    blank_weight = jnp.where(active_frame & (token_pos <= token_len)[None, :], blanks, 0.0)
    label_weight = jnp.where(active_frame & (token_pos < token_len)[None, :], labels, 0.0)
    return (blank_weight.reshape(-1), label_weight.reshape(-1))


def logit_grad(logits, log_total, blank_weight, label_weight, cell_targets):
    prob = jnp.exp(logits - log_total[:, None])
    vocab = jnp.arange(logits.shape[1], dtype=jnp.int32)
    grad = (blank_weight + label_weight)[:, None] * prob
    grad = grad - jnp.where(vocab[None, :] == 0, blank_weight[:, None], 0.0)
    grad = grad - jnp.where(vocab[None, :] == cell_targets[:, None], label_weight[:, None], 0.0)
    return grad.astype(jnp.bfloat16)


def cell_backward(hidden, grad_hidden):
    hidden_full = hidden.astype(jnp.float32)
    return grad_hidden * (1.0 - hidden_full * hidden_full)


def contract_rows(left, right):
    return lax.dot_general(
        left, right, (((0,), (0,)), ((), ())), preferred_element_type=jnp.float32
    )


def contract_cols(left, right):
    return lax.dot_general(
        left, right, (((1,), (1,)), ((), ())), preferred_element_type=jnp.float32
    )


def exact_rows(left, right):
    return lax.dot_general(
        left,
        right,
        (((0,), (0,)), ((), ())),
        precision=lax.Precision.HIGHEST,
        preferred_element_type=jnp.float32,
    )


def pick_unit(stacked, unit_index):
    return lax.dynamic_index_in_dim(stacked, unit_index, 0, keepdims=False)


def local(
    encoder_out,
    predictor_out,
    enc_weight,
    pred_weight,
    joint_bias,
    out_weight,
    blank_occupancy,
    label_occupancy,
    frame_lengths,
    token_lengths,
    target_ids,
):
    joint_width = enc_weight.shape[1]
    vocab_size = out_weight.shape[1]
    tile_frames = blank_occupancy.shape[1]
    tile_tokens = blank_occupancy.shape[2]
    batch_index = lax.axis_index("batch")
    frame_index = lax.axis_index("frame")
    token_index = lax.axis_index("token")
    first_frame = frame_index * tile_frames
    first_token = token_index * tile_tokens
    enc_full = lax.all_gather(encoder_out, "token", axis=2, tiled=True)[0]
    pred_full = lax.all_gather(predictor_out, "frame", axis=2, tiled=True)[0]
    enc_proj = jnp.dot(enc_full, enc_weight, preferred_element_type=jnp.float32)
    pred_proj = jnp.dot(pred_full, pred_weight, preferred_element_type=jnp.float32)
    blank_tile = blank_occupancy[0]
    label_tile = label_occupancy[0]
    own_targets = pick_unit(target_ids, batch_index)
    own_frames = pick_unit(frame_lengths, batch_index)
    own_tokens = pick_unit(token_lengths, batch_index)
    unit_rows = enc_proj[None]
    unit_pred = pred_proj[None]
    unit_blank = blank_tile[None]
    unit_label = label_tile[None]
    unit_targets = own_targets[None]
    unit_frames = own_frames[None]
    unit_tokens = own_tokens[None]
    unit_count = unit_rows.shape[0]
    unit_length = unit_rows.shape[1]
    blocks = unit_length // FB

    def block_inputs(block_index):
        unit_index = block_index // blocks
        first_row = block_index % blocks * FB
        frame_rows = lax.dynamic_slice_in_dim(pick_unit(unit_rows, unit_index), first_row, FB, 0)
        blanks = lax.dynamic_slice_in_dim(pick_unit(unit_blank, unit_index), first_row, FB, 0)
        labels = lax.dynamic_slice_in_dim(pick_unit(unit_label, unit_index), first_row, FB, 0)
        frame_len = pick_unit(unit_frames, unit_index)
        token_len = pick_unit(unit_tokens, unit_index)
        hidden = cell_hidden(frame_rows, pick_unit(unit_pred, unit_index), joint_bias)
        frame_start = first_frame + first_row
        blank_weight, label_weight = cell_weights(
            blanks, labels, frame_start, first_token, frame_len, token_len
        )
        cell_targets = jnp.tile(pick_unit(unit_targets, unit_index), FB)
        active_block = (frame_start < frame_len) & (first_token <= token_len)
        return (
            unit_index,
            first_row,
            hidden,
            blank_weight,
            label_weight,
            cell_targets,
            active_block,
        )

    def row_step(block_index, totals):
        grad_out, grad_pred, grad_bias, grad_rows = totals
        unit_index, first_row, hidden, blank_weight, label_weight, cell_targets, active_block = (
            block_inputs(block_index)
        )

        def work_block(operand):
            logits = jnp.dot(hidden, out_weight, preferred_element_type=jnp.float32)
            log_total = jnp.log(jnp.sum(jnp.exp(logits), axis=1))
            grad_logits = logit_grad(logits, log_total, blank_weight, label_weight, cell_targets)
            grad_hidden = contract_cols(grad_logits, out_weight)
            grad_inner = cell_backward(hidden, grad_hidden).reshape(FB, tile_tokens, joint_width)
            return (
                contract_rows(hidden, grad_logits),
                grad_inner.sum(0),
                grad_inner.sum((0, 1)),
                grad_inner.sum(1),
            )

        def empty_block(operand):
            return (
                jnp.zeros((joint_width, vocab_size), jnp.float32),
                jnp.zeros((tile_tokens, joint_width), jnp.float32),
                jnp.zeros((joint_width,), jnp.float32),
                jnp.zeros((FB, joint_width), jnp.float32),
            )

        block_terms = lax.cond(active_block, work_block, empty_block, 0)
        grad_rows = lax.dynamic_update_slice(
            grad_rows, block_terms[3][None], (unit_index, first_row, jnp.int32(0))
        )
        return (
            grad_out + block_terms[0],
            grad_pred.at[unit_index].add(block_terms[1]),
            grad_bias + block_terms[2],
            grad_rows,
        )

    start = (
        jnp.zeros((joint_width, vocab_size), jnp.float32),
        jnp.zeros((unit_count, tile_tokens, joint_width), jnp.float32),
        jnp.zeros((joint_width,), jnp.float32),
        jnp.zeros((unit_count, unit_length, joint_width), jnp.float32),
    )
    grad_out, grad_pred, grad_bias, grad_rows = lax.fori_loop(
        0, unit_count * blocks, row_step, start
    )
    out_wgrad, bias_share = (
        lax.psum_scatter(grad_out, ("frame", "token", "batch"), scatter_dimension=0, tiled=True),
        lax.psum_scatter(grad_bias, ("frame", "token", "batch"), scatter_dimension=0, tiled=True),
    )
    enc_rows_grad = grad_rows[0]
    pred_rows_grad = grad_pred[0]
    enc_term = jnp.dot(
        enc_rows_grad, enc_weight.astype(jnp.float32).T, precision=lax.Precision.HIGHEST
    )
    pred_term = jnp.dot(
        pred_rows_grad, pred_weight.astype(jnp.float32).T, precision=lax.Precision.HIGHEST
    )
    enc_grad = lax.psum_scatter(enc_term[None], "token", scatter_dimension=2, tiled=True)
    pred_grad = lax.psum_scatter(pred_term[None], "frame", scatter_dimension=2, tiled=True)
    enc_wterm = exact_rows(enc_full.astype(jnp.float32), enc_rows_grad)
    pred_wterm = exact_rows(pred_full.astype(jnp.float32), pred_rows_grad)
    enc_wgrad, pred_wgrad = (
        lax.psum_scatter(enc_wterm, ("frame", "token", "batch"), scatter_dimension=0, tiled=True),
        lax.psum_scatter(pred_wterm, ("frame", "token", "batch"), scatter_dimension=0, tiled=True),
    )
    return (enc_grad, pred_grad, enc_wgrad, pred_wgrad, out_wgrad, bias_share)


def solution(mesh):
    in_specs = (
        P("batch", "frame", "token"),
        P("batch", "token", "frame"),
        P(),
        P(),
        P(),
        P(),
        P("batch", "frame", "token"),
        P("batch", "frame", "token"),
        P(),
        P(),
        P(None, "token"),
    )
    out_specs = (
        P("batch", "frame", "token"),
        P("batch", "token", "frame"),
        P(("frame", "token", "batch"), None),
        P(("frame", "token", "batch"), None),
        P(("frame", "token", "batch"), None),
        P(("frame", "token", "batch")),
    )
    return jax.shard_map(local, mesh=mesh, in_specs=in_specs, out_specs=out_specs, check_vma=False)
```

profile of v0, /device:TPU:1, one launch (start us, length us, event | category | flops | bytes accessed | tf_op | source)
XLA Modules:
  0.0 406.6 jit_solution(7293785015536965852)
XLA Ops:
  8.1 1.4 dynamic_slice.56
  13.5 31.0 %all_gather.7 = bf16[1,64,512]{1,0,2:T(2,128)(2,1)S(1)} all-gather(bf16[1,64,64]{1,0,2:T(2,128)(2,1)S(1)} %copy.27), channel_id=1, replica_groups=mesh['frame'=8,'token'=8,'batch'=2] {'frame'}, dimensions={2}, use_global_device_ids=true | all-gather | bytes 73728 | tf_op jit(solution)/shard_map/all_gather | solution.py:86
  44.7 22.9 %all_gather.6 = bf16[1,64,512]{1,0,2:T(2,128)(2,1)S(1)} all-gather(bf16[1,64,64]{1,0,2:T(2,128)(2,1)S(1)} %copy.25), channel_id=1, replica_groups=mesh['frame'=8,'token'=8,'batch'=2] {'token'}, dimensions={2}, use_global_device_ids=true | all-gather | bytes 73728 | tf_op jit(solution)/shard_map/all_gather | solution.py:85
  71.2 146.4 %while.23 = (s32[]{:T(128)}, f32[512,1024]{0,1:T(8,128)}, f32[1,64,512]{2,1,0:T(8,128)S(1)}, f32[512]{0:T(512)}, f32[1,64,512]{2,1,0:T(8,128)}, /*index=5*/s32[]...) while((s32[]{:T(128)}, f32[512,1024]{0,1:T(8,128)}, ...), condition=%wide.region_8.9_spmd.clone, body=%wide.region_0.8_spmd.clone.sunk | while | flops 1619066624 | bytes 34392368 | solution.py:174
  74.3 10.0 %conditional.3 = (f32[512,1024]{0,1:T(8,128)S(1)}, f32[512]{0:T(512)}, f32[1,64,512]{2,1,0:T(8,128)S(1)}, f32[1,8,512]{2,1,0:T(8,128)S(1)}) conditional(s32[]{:T(128)} %convert_element_type.47, () %tuple.109, (s32[]{:T(128)}, s32[8]{0:T(128)S(1)}, s32[]{:T(128)}, s32[]{:T(128)}, s32[64]{0:T(128)S(1)}, /*index=5*/s32[1]{0:T(128)}, ...), branch_computations={%region_1.1_spmd, %region_2.6_spmd} | conditional | flops 1617132288 | bytes 24847264 | solution.py:157
  77.5 2.0 exponential_reduce_fusion
  82.3 2.0 convolution_bitcast_fusion
  84.3 1.9 select_add_fusion.4
  91.2 10.0 %conditional.3 = (f32[512,1024]{0,1:T(8,128)S(1)}, f32[512]{0:T(512)}, f32[1,64,512]{2,1,0:T(8,128)S(1)}, f32[1,8,512]{2,1,0:T(8,128)S(1)}) conditional(s32[]{:T(128)} %convert_element_type.47, () %tuple.109, (s32[]{:T(128)}, s32[8]{0:T(128)S(1)}, s32[]{:T(128)}, s32[]{:T(128)}, s32[64]{0:T(128)S(1)}, /*index=5*/s32[1]{0:T(128)}, ...), branch_computations={%region_1.1_spmd, %region_2.6_spmd} | conditional | flops 1617132288 | bytes 24847264 | solution.py:157
  94.4 2.0 exponential_reduce_fusion
  99.2 2.0 convolution_bitcast_fusion
  101.2 3.4 select_add_fusion.4
  109.7 10.0 %conditional.3 = (f32[512,1024]{0,1:T(8,128)S(1)}, f32[512]{0:T(512)}, f32[1,64,512]{2,1,0:T(8,128)S(1)}, f32[1,8,512]{2,1,0:T(8,128)S(1)}) conditional(s32[]{:T(128)} %convert_element_type.47, () %tuple.109, (s32[]{:T(128)}, s32[8]{0:T(128)S(1)}, s32[]{:T(128)}, s32[]{:T(128)}, s32[64]{0:T(128)S(1)}, /*index=5*/s32[1]{0:T(128)}, ...), branch_computations={%region_1.1_spmd, %region_2.6_spmd} | conditional | flops 1617132288 | bytes 24847264 | solution.py:157
  112.9 2.0 exponential_reduce_fusion
  117.7 2.0 convolution_bitcast_fusion
  119.7 3.4 select_add_fusion.4
  128.2 10.0 %conditional.3 = (f32[512,1024]{0,1:T(8,128)S(1)}, f32[512]{0:T(512)}, f32[1,64,512]{2,1,0:T(8,128)S(1)}, f32[1,8,512]{2,1,0:T(8,128)S(1)}) conditional(s32[]{:T(128)} %convert_element_type.47, () %tuple.109, (s32[]{:T(128)}, s32[8]{0:T(128)S(1)}, s32[]{:T(128)}, s32[]{:T(128)}, s32[64]{0:T(128)S(1)}, /*index=5*/s32[1]{0:T(128)}, ...), branch_computations={%region_1.1_spmd, %region_2.6_spmd} | conditional | flops 1617132288 | bytes 24847264 | solution.py:157
  131.4 2.0 exponential_reduce_fusion
  136.2 2.0 convolution_bitcast_fusion
  138.2 3.4 select_add_fusion.4
  146.6 10.0 %conditional.3 = (f32[512,1024]{0,1:T(8,128)S(1)}, f32[512]{0:T(512)}, f32[1,64,512]{2,1,0:T(8,128)S(1)}, f32[1,8,512]{2,1,0:T(8,128)S(1)}) conditional(s32[]{:T(128)} %convert_element_type.47, () %tuple.109, (s32[]{:T(128)}, s32[8]{0:T(128)S(1)}, s32[]{:T(128)}, s32[]{:T(128)}, s32[64]{0:T(128)S(1)}, /*index=5*/s32[1]{0:T(128)}, ...), branch_computations={%region_1.1_spmd, %region_2.6_spmd} | conditional | flops 1617132288 | bytes 24847264 | solution.py:157
  149.9 2.0 exponential_reduce_fusion
  154.7 2.0 convolution_bitcast_fusion
  156.7 3.4 select_add_fusion.4
  165.1 10.0 %conditional.3 = (f32[512,1024]{0,1:T(8,128)S(1)}, f32[512]{0:T(512)}, f32[1,64,512]{2,1,0:T(8,128)S(1)}, f32[1,8,512]{2,1,0:T(8,128)S(1)}) conditional(s32[]{:T(128)} %convert_element_type.47, () %tuple.109, (s32[]{:T(128)}, s32[8]{0:T(128)S(1)}, s32[]{:T(128)}, s32[]{:T(128)}, s32[64]{0:T(128)S(1)}, /*index=5*/s32[1]{0:T(128)}, ...), branch_computations={%region_1.1_spmd, %region_2.6_spmd} | conditional | flops 1617132288 | bytes 24847264 | solution.py:157
  168.3 2.0 exponential_reduce_fusion
  173.2 2.0 convolution_bitcast_fusion
  175.2 3.4 select_add_fusion.4
  183.6 10.0 %conditional.3 = (f32[512,1024]{0,1:T(8,128)S(1)}, f32[512]{0:T(512)}, f32[1,64,512]{2,1,0:T(8,128)S(1)}, f32[1,8,512]{2,1,0:T(8,128)S(1)}) conditional(s32[]{:T(128)} %convert_element_type.47, () %tuple.109, (s32[]{:T(128)}, s32[8]{0:T(128)S(1)}, s32[]{:T(128)}, s32[]{:T(128)}, s32[64]{0:T(128)S(1)}, /*index=5*/s32[1]{0:T(128)}, ...), branch_computations={%region_1.1_spmd, %region_2.6_spmd} | conditional | flops 1617132288 | bytes 24847264 | solution.py:157
  186.8 2.0 exponential_reduce_fusion
  190.1 1.3 fusion.11
  191.7 2.0 convolution_bitcast_fusion
  193.7 3.4 select_add_fusion.4
  202.1 10.0 %conditional.3 = (f32[512,1024]{0,1:T(8,128)S(1)}, f32[512]{0:T(512)}, f32[1,64,512]{2,1,0:T(8,128)S(1)}, f32[1,8,512]{2,1,0:T(8,128)S(1)}) conditional(s32[]{:T(128)} %convert_element_type.47, () %tuple.109, (s32[]{:T(128)}, s32[8]{0:T(128)S(1)}, s32[]{:T(128)}, s32[]{:T(128)}, s32[64]{0:T(128)S(1)}, /*index=5*/s32[1]{0:T(128)}, ...), branch_computations={%region_1.1_spmd, %region_2.6_spmd} | conditional | flops 1617132288 | bytes 24847264 | solution.py:157
  205.3 2.0 exponential_reduce_fusion
  210.2 2.0 convolution_bitcast_fusion
  212.1 3.4 select_add_fusion.4
  217.6 2.3 convolution_bitcast_fusion.4
  220.0 2.3 convolution_bitcast_fusion.3
  222.4 1.6 convolution_bitcast_fusion.1
  224.0 1.9 copy.29
  225.9 1.6 convolution_bitcast_fusion.2
  228.2 76.8 %all-reduce.3 = f32[512]{0:T(512)S(1)} all-reduce(f32[512]{0:T(512)S(1)} %copy-done.11), channel_id=7, replica_groups=mesh['frame'=8,'token'=8,'batch'=2] {'frame','token','batch'}, use_global_device_ids=true, to_apply=%region_14.15.clone | all-reduce | flops 512 | bytes 4096
  305.6 1.5 copy.33
  307.1 32.4 %reduce-scatter.11.cloned.1.call-done = f32[64,64]{1,0:T(8,128)} async-done(((f32[512,64]{1,0:T(8,128)}), f32[64,64]{1,0:T(8,128)}) %reduce-scatter.11.cloned.1.call-update) | async-done | bytes 16400
  339.4 1.5 copy.35
  340.9 54.2 %all-reduce.7.cloned.1.call-done = (f32[512,512]{0,1:T(8,128)}, f32[512,512]{0,1:T(8,128)}, f32[512,1024]{1,0:T(8,128)}) async-done(((f32[512,512]{0,1:T(8,128)}, f32[512,512]{0,1:T(8,128)}, f32[512,1024]{1,0:T(8,128)}), (f32[512,512]{0,1:T(8,128)}, f32[512,512]{0,1:T(8,128)}, f32[512,1024]{1,0:T(8,128)})) %all-reduce.7.cloned.1.call-update) | async-done | bytes 4194320
  395.1 1.4 constant_dynamic-slice_fusion.2
  (310 shorter events, 91.9 us)
Async XLA Ops:
  8.0 61.7 %copy-start = (bf16[512,512]{1,0:T(8,128)(2,1)S(1)}, bf16[512,512]{1,0:T(8,128)(2,1)}, u32[]{:S(2)}) copy-start(bf16[512,512]{1,0:T(8,128)(2,1)} %param.19) | copy-start | bytes 1572868
  8.0 297.6 %reduce-scatter.9.cloned.1.call-start = ((), (), s32[]{:S(2)}) async-start(), calls=%async_computation.2 | async-start | bytes 294912
  44.7 26.5 %copy-start.7 = (bf16[1,64,512]{2,1,0:T(8,128)(2,1)}, bf16[1,64,512]{2,1,0:T(8,128)(2,1)S(1)}, u32[]{:S(2)}) copy-start(bf16[1,64,512]{2,1,0:T(8,128)(2,1)S(1)} %copy.28) | copy-start | bytes 196612
  67.7 3.5 copy-start.5
  79.5 1.2 copy-start.3
  80.7 1.4 copy-start.1
  84.3 1.9 copy-start.9
  86.8 1.3 copy-start.10
  96.4 1.2 copy-start.3
  97.6 1.3 copy-start.1
  101.2 3.5 copy-start.9
  105.3 1.3 copy-start.10
  114.9 1.2 copy-start.3
  116.1 1.3 copy-start.1
  119.7 3.5 copy-start.9
  123.8 1.3 copy-start.10
  133.4 1.2 copy-start.3
  134.6 1.3 copy-start.1
  138.2 3.5 copy-start.9
  142.3 1.3 copy-start.10
  151.9 1.2 copy-start.3
  153.1 1.3 copy-start.1
  156.6 3.5 copy-start.9
  160.8 1.3 copy-start.10
  170.4 1.2 copy-start.3
  171.6 1.3 copy-start.1
  175.1 3.5 copy-start.9
  179.3 1.3 copy-start.10
  188.9 1.2 copy-start.3
  190.1 1.4 copy-start.1
  193.6 3.5 copy-start.9
  197.8 1.3 copy-start.10
  207.4 1.2 copy-start.3
  208.6 1.3 copy-start.1
  212.1 3.5 copy-start.9
  216.3 1.3 copy-start.10
  217.6 4.8 %copy-start.8 = (bf16[1,64,512]{2,1,0:T(8,128)(2,1)S(1)}, bf16[1,64,512]{2,1,0:T(8,128)(2,1)}, u32[]{:S(2)}) copy-start(bf16[1,64,512]{2,1,0:T(8,128)(2,1)} %copy-done.7) | copy-start | bytes 196612
  217.6 6.4 %copy-start.2 = (f32[512,1024]{0,1:T(8,128)S(1)}, f32[512,1024]{0,1:T(8,128)}, u32[]{:S(2)}) copy-start(f32[512,1024]{0,1:T(8,128)} %get-tuple-element.624) | copy-start | bytes 6291460
  219.9 119.5 %reduce-scatter.11.cloned.1.call-start = ((), (), s32[]{:S(2)}) async-start(), calls=%async_computation.3 | async-start | bytes 294912
  222.3 172.8 %all-reduce.7.cloned.1.call-start = ((), (), s32[]{:S(2)}) async-start(), calls=%async_computation.4 | async-start | bytes 8388608
  224.0 1.9 copy-start.4
  224.0 1.9 copy-start.6
  227.5 0.7 copy-start.11
Sparse Core Ops, SparseCore 0:
  220.1 43.2 reduce-scatter.8
  267.3 72.1 reduce-scatter.10
Sparse Core Ops, SparseCore 1:
  229.1 165.9 all-reduce.6
where the time goes:
time: 410 us; the launch traced here: 407 us
  blocking collectives  131 us (32%)
  waiting for transfers between devices  86.6 us (21%)
  other arithmetic  70.7 us (17%)
  matrix products  52.8 us (13%)
  local copies, waits for them, and re-layouts  43.1 us (11%)
  between operations  16.3 us (4%)
  loops' own time  6.18 us (2%)
    unnamed x6, waiting for transfers between devices  86.6 us
    unnamed x1, blocking collectives  76.8 us
    all_gather x1, blocking collectives, local(): pred_full = lax.all_gather(predictor_out, 'frame', axis=2, tiled=True)[0]  31 us
    add x8, other arithmetic, row_step(): grad_out + block_terms[0]  26 us
    all_gather x1, blocking collectives, local(): enc_full = lax.all_gather(encoder_out, 'token', axis=2, tiled=True)[0]  22.9 us
    dot_general x8, matrix products, work_block(): logits = jnp.dot(hidden, out_weight, preferred_element_type=jnp.float32)  16.3 us
    dot_general x8, matrix products, contract_rows(): lax.dot_general(left, right, (((0,), (0,)), ((), ())), preferred_element_...  15.7 us
    dot_general x8, matrix products, contract_cols(): lax.dot_general(left, right, (((1,), (1,)), ((), ())), preferred_element_...  10.8 us
  transfers between devices with their start and end apart: 3, of which 2 were waited for; matrix products, arithmetic and copies ran while one was open for 3% of the time, Pallas kernels for 0%

commit v1 on v0

v1 whole, which is shorter than its diff:
```python
import jax
import jax.numpy as jnp
from jax import lax
from jax.experimental import pallas as pl
from jax.experimental.pallas import tpu as pltpu
from jax.sharding import PartitionSpec as P

FB = 16
CHUNK = 256
BIG = 63 * 1024 * 1024
ALL = ("frame", "token", "batch")
F32, BF16 = jnp.float32, jnp.bfloat16


def split3(x):
    hi = x.astype(BF16)
    rest = x - hi.astype(F32)
    mid = rest.astype(BF16)
    lo = (rest - mid.astype(F32)).astype(BF16)
    return hi, mid, lo


def dot_nt(a, b):
    return lax.dot_general(a, b, (((1,), (1,)), ((), ())), preferred_element_type=F32)


def dot_tn(a, b):
    return lax.dot_general(a, b, (((0,), (0,)), ((), ())), preferred_element_type=F32)


def exact_nt(a, b):
    return sum(dot_nt(piece, b) for piece in split3(a))


def exact_tn(a, b):
    return sum(dot_tn(a, piece) for piece in split3(b))


def cells_kernel(
    g_hbm, h_hbm, encw_hbm, predw_hbm, bias_hbm, blank_hbm, label_hbm, tgt_hbm, flen_hbm, tlen_hbm, ow_hbm,
    keep_ref, send_ref, stash_hbm,
    g_ref, h_ref, encw_ref, predw_ref, bias_ref, blank_ref, label_ref, tgt_ref, flen_ref, tlen_ref, ow_ref,
    sems, out_sems, encp_ref, predp_ref, rows_ref, prow_ref, bw_ref, lw_ref, tgt_col_ref, e_ref, stash_ref,
):
    nf, nt = blank_ref.shape[1], blank_ref.shape[2]
    joint, vocab = ow_ref.shape
    parts, width = g_ref.shape[0], g_ref.shape[2] // 2
    cells = FB * nt
    core = lax.axis_index("batch")
    first = core == 0
    hbm = [g_hbm, h_hbm, encw_hbm, predw_hbm, bias_hbm, blank_hbm, label_hbm, tgt_hbm, flen_hbm, tlen_hbm, ow_hbm]
    here = [g_ref, h_ref, encw_ref, predw_ref, bias_ref, blank_ref, label_ref, tgt_ref, flen_ref, tlen_ref, ow_ref]
    copies = [pltpu.make_async_copy(src, dst, sems.at[i]) for i, (src, dst) in enumerate(zip(hbm, here))]
    for copy in copies:
        copy.start()
    for copy in copies[:-1]:
        copy.wait()
    frame_len = flen_ref[core]
    token_len = tlen_ref[core]
    first_frame = lax.axis_index("frame") * nf
    first_token = lax.axis_index("token") * nt

    encp = jnp.zeros((nf, joint), F32)
    predp = jnp.zeros((nt, joint), F32)
    for s in range(parts):
        own = g_ref[s][:, :width]
        other = h_ref[s][:, width:]
        rows = slice(s * width, (s + 1) * width)
        encp += jnp.dot(jnp.where(first, own, other), encw_ref[rows, :], preferred_element_type=F32)
        predp += jnp.dot(jnp.where(first, other, own), predw_ref[rows, :], preferred_element_type=F32)
    encp_ref[...] = encp
    predp_ref[...] = predp + bias_ref[...]

    frame_pos = first_frame + lax.broadcasted_iota(jnp.int32, (nf, nt), 0)
    token_pos = first_token + lax.broadcasted_iota(jnp.int32, (nf, nt), 1)
    live = frame_pos < frame_len
    bw_ref[...] = jnp.where(live & (token_pos <= token_len), blank_ref[0], 0.0)
    lw_ref[...] = jnp.where(live & (token_pos < token_len), label_ref[0], 0.0)
    diag = lax.broadcasted_iota(jnp.int32, (nt, nt), 0) == lax.broadcasted_iota(jnp.int32, (nt, nt), 1)
    targets = jnp.where(first, tgt_ref[0:1, :], tgt_ref[1:2, :]).astype(F32)
    tgt_col = jnp.sum(jnp.where(diag, targets, 0.0), axis=1, keepdims=True).astype(jnp.int32)
    tgt_col_ref[...] = jnp.broadcast_to(tgt_col, (nt, 128))
    prow_ref[...] = jnp.zeros_like(prow_ref)
    lane = lax.broadcasted_iota(jnp.int32, (FB, nt, 128), 2)
    copies[-1].wait()

    def columns(ref, t0):
        rows = ref[pl.ds(t0, FB), :]
        return jnp.sum(jnp.where(diag[None], rows[:, None, :], 0.0), axis=2, keepdims=True)

    def block(i, carry):
        t0 = pl.multiple_of(i * FB, FB)
        span = pl.ds(pl.multiple_of(i * cells, cells), cells)
        frames = encp_ref[pl.ds(t0, FB), :]
        inner = frames[:, None, :] + predp_ref[...][None, :, :]
        hidden = jnp.tanh(inner).astype(BF16).reshape(cells, joint)
        stash_ref[span, :joint] = hidden
        total = jnp.zeros((cells, 128), F32)
        for c in range(vocab // CHUNK):
            cols = slice(c * CHUNK, (c + 1) * CHUNK)
            e = jnp.exp(jnp.dot(hidden, ow_ref[:, cols], preferred_element_type=F32))
            e_ref[:, cols] = e
            for q in range(CHUNK // 128):
                total = total + e[:, q * 128 : (q + 1) * 128]
        total = jnp.sum(total, axis=1, keepdims=True).reshape(FB, nt, 1)
        bw = columns(bw_ref, t0)
        lw = columns(lw_ref, t0)
        scale = (bw + lw) / total
        tgt = tgt_col_ref[...][None]
        for v in range(vocab // 128):
            cols = slice(v * 128, (v + 1) * 128)
            g = e_ref[:, cols].reshape(FB, nt, 128) * scale
            if v == 0:
                g = g - jnp.where(lane == 0, bw, 0.0)
            g = g - jnp.where(lane == tgt - v * 128, lw, 0.0)
            stash_ref[span, joint + v * 128 : joint + (v + 1) * 128] = g.astype(BF16).reshape(cells, 128)
        pltpu.make_async_copy(stash_ref.at[span], stash_hbm.at[span], out_sems.at[i]).start()
        for c in range(joint // CHUNK):
            cols = slice(c * CHUNK, (c + 1) * CHUNK)
            grad_hidden = dot_nt(stash_ref[span, joint:], ow_ref[cols, :])
            hf = stash_ref[span, cols].astype(F32)
            gi = (grad_hidden * (1.0 - hf * hf)).reshape(FB, nt, CHUNK)
            prow_ref[:, cols] += gi.sum(0)
            rows_ref[pl.ds(t0, FB), cols] = gi.sum(1)
        return carry

    lax.fori_loop(0, nf // FB, block, 0)

    term_e = exact_nt(rows_ref[...], encw_ref[...])
    term_p = exact_nt(prow_ref[...], predw_ref[...])
    for s in range(parts):
        cols = slice(s * width, (s + 1) * width)
        e_part = jnp.concatenate([term_e[:, cols], rows_ref[:, cols]], axis=1)
        p_part = jnp.concatenate([term_p[:, cols], prow_ref[:, cols]], axis=1)
        keep_ref[s] = jnp.where(first, e_part, p_part)
        send_ref[s] = jnp.where(first, p_part, e_part)
    for i in range(nf // FB):
        span = pl.ds(i * cells, cells)
        pltpu.make_async_copy(stash_ref.at[span], stash_hbm.at[span], out_sems.at[i]).wait()


def wgrad_kernel(stash_hbm, g_ref, h_ref, keep_ref, send_ref, feat_ref, stash_ref, acc_ref, sems):
    parts, nt, two = g_ref.shape
    width = two // 2
    joint, vocab = acc_ref.shape
    first = lax.axis_index("batch") == 0
    steps = sems.shape[0]
    step = stash_ref.shape[0] // steps
    for i in range(steps):
        span = pl.ds(i * step, step)
        pltpu.make_async_copy(stash_hbm.at[span], stash_ref.at[span], sems.at[i]).start()
    for s in range(parts):
        for is_enc in (True, False):
            x = jnp.where(first == is_enc, g_ref[s], h_ref[s]).astype(F32)
            feat_ref[0 if is_enc else 1, s * width : (s + 1) * width, :] = jnp.concatenate(
                [x[:, :width].T, x[:, width:].T], axis=1
            ).astype(BF16)
    acc_ref[...] = jnp.zeros_like(acc_ref)

    def block(i, carry):
        span = pl.ds(pl.multiple_of(i * step, step), step)
        pltpu.make_async_copy(stash_hbm.at[span], stash_ref.at[span], sems.at[i]).wait()
        acc_ref[...] += dot_tn(stash_ref[span, :joint], stash_ref[span, joint:])
        return carry

    lax.fori_loop(0, steps, block, 0)

    chips = joint // 8
    top = lax.broadcasted_iota(jnp.int32, (chips, 8, 128), 1) < 4
    for v in range(vocab // 256):
        a = acc_ref[:, v * 256 : v * 256 + 128].reshape(chips, 8, 128)
        b = acc_ref[:, v * 256 + 128 : v * 256 + 256].reshape(chips, 8, 128)
        upper = jnp.where(top, a, pltpu.roll(b, 4, 1))
        lower = jnp.where(top, pltpu.roll(a, 4, 1), b)
        rows = slice(v * 8, v * 8 + 8)
        keep_ref[:, rows, :] = jnp.where(first, upper, lower)
        send_ref[:, rows, :] = jnp.where(first, lower, upper)


LEVELS = 32000.0
STEPS = 16.0


def pack_kernel(keep_ref, recv_ref, own_ref, partner_ref, feat_ref, out_ref, small_ref):
    chips, rows, _ = keep_ref.shape
    two = own_ref.shape[1]
    width = two // 2
    core = lax.axis_index("batch")
    first = core == 0
    own, partner = own_ref[:, width:], partner_ref[:, width:]
    enc_rows = jnp.where(first, own, partner)
    pred_rows = jnp.where(first, partner, own)
    parts = []
    for i, value in enumerate((enc_rows, pred_rows)):
        parts.append(sum(jnp.dot(feat_ref[i], piece, preferred_element_type=F32) for piece in split3(value)))
    weights = jnp.concatenate(parts, axis=1).reshape(chips, 8, two)
    weights = jnp.where(first, weights, pltpu.roll(weights, 4, 1))
    bias = jnp.sum(enc_rows, axis=0, keepdims=True)
    bias = jnp.concatenate([bias, jnp.zeros_like(bias)], axis=1)[None]
    sub = lax.broadcasted_iota(jnp.int32, (chips, 8, two), 1)
    small_ref[...] = jnp.where(sub < 4, weights, jnp.where(sub == 4, bias, 0.0))

    batch = 16
    total = rows + 8
    diag = lax.broadcasted_iota(jnp.int32, (batch, total, 128), 1) == lax.broadcasted_iota(
        jnp.int32, (batch, total, 128), 2
    )
    for i in range(0, chips, batch):
        part = slice(i, i + batch)
        x = jnp.concatenate([keep_ref[part] + recv_ref[part], small_ref[part]], axis=1)
        largest = jnp.maximum(jnp.max(jnp.abs(x), axis=2, keepdims=True), 1e-30)
        power = jnp.ceil(jnp.log2(largest) * STEPS)
        q = jnp.round(x * (LEVELS * jnp.exp2(power * (-1.0 / STEPS))))
        powers = jnp.sum(jnp.where(diag, power, 0.0), axis=1, keepdims=True)
        tail = jnp.broadcast_to(powers, (batch, 8, 128))
        out_ref[part] = jnp.concatenate([q, tail], axis=1).astype(jnp.int32).astype(jnp.int16)


def last_kernel(z_ref, own_ref, partner_ref, enc_ref, pred_ref, encw_ref, predw_ref, outw_ref, bias_ref):
    core = lax.axis_index("batch")
    first = core == 0
    frame = lax.axis_index("frame")
    rows = z_ref.shape[1] - 8
    big = rows - 8
    n = 8
    width = own_ref.shape[1] // 2
    row = lax.broadcasted_iota(jnp.int32, (rows, 128), 0)
    lane = lax.broadcasted_iota(jnp.int32, (rows, 128), 1)
    diag = row == lane
    total = jnp.zeros((big, 128), F32)
    by_token = [jnp.zeros((8, 128), F32)] * n
    by_frame = [jnp.zeros((8, 128), F32)] * n
    for f in range(n):
        for k in range(n):
            x = z_ref[f * n + k].astype(jnp.int32).astype(F32)
            power = jnp.sum(jnp.where(diag, x[rows : rows + 1], 0.0), axis=1, keepdims=True)
            x = x[:rows] * (jnp.exp2(power * (1.0 / STEPS)) * (1.0 / LEVELS))
            total = total + x[:big]
            by_token[k] = by_token[k] + x[big:]
            by_frame[f] = by_frame[f] + x[big:]
    for v in range(big // 4):
        outw_ref[:, v * 128 : (v + 1) * 128] = total[v * 4 : v * 4 + 4, :]
    bias = jnp.zeros((1, 128), F32)
    for j in range(n):
        cols = slice(j * width, (j + 1) * width)
        encw_ref[:, cols] = by_token[j][:4, :width]
        predw_ref[:, cols] = by_frame[j][:4, width:]
        bias = bias + jnp.where(frame == j, by_token[j][4:5], 0.0)
    offset = lax.axis_index("token") * 8 + core * 4
    bias_ref[...] = pltpu.roll(bias, 128 - offset, 1)[:, :4]
    nt = enc_ref.shape[1]
    own, other = own_ref[:nt, :width], partner_ref[nt:, :width]
    enc_ref[0] = jnp.where(first, own, other)
    pred_ref[0] = jnp.where(first, other, own)


VM = pl.BlockSpec(memory_space=pltpu.VMEM)
HBM = pl.BlockSpec(memory_space=pl.ANY)


def shape(*dims):
    return jax.ShapeDtypeStruct(dims, F32)


def local(
    encoder_out, predictor_out, enc_weight, pred_weight, joint_bias, out_weight,
    blank_occupancy, label_occupancy, frame_lengths, token_lengths, target_ids,
):
    joint, vocab = out_weight.shape
    nf, nt = blank_occupancy.shape[1:]
    width = encoder_out.shape[2]
    core = lax.axis_index("batch")
    n = lax.axis_size("frame")
    groups = [[f * 2 * n + k * 2 for k in range(n)] for f in range(n)]
    groups += [[f * 2 * n + k * 2 + 1 for f in range(n)] for k in range(n)]

    def swap(x):
        return lax.ppermute(x, "batch", [(0, 1), (1, 0)])

    def exchange(x):
        return lax.all_to_all(x, ALL, 0, 0, axis_index_groups=groups)

    enc, pred = encoder_out[0], predictor_out[0]
    keep = jnp.where(core == 0, enc, pred)
    recv = swap(jnp.where(core == 0, pred, enc))
    pair = jnp.concatenate([keep, recv], axis=1)
    gathered = exchange(jnp.broadcast_to(pair[None], (n, nf, 2 * width)))
    partner = swap(gathered)

    cells = nf * nt
    block = FB * nt
    arrays = (gathered, partner, enc_weight, pred_weight, joint_bias[None], blank_occupancy, label_occupancy, target_ids)
    lengths = (frame_lengths, token_lengths)
    term_keep, term_send, stash = pl.pallas_call(
        cells_kernel,
        out_shape=[
            shape(n, nf, 2 * width), shape(n, nf, 2 * width), jax.ShapeDtypeStruct((cells, joint + vocab), BF16),
        ],
        in_specs=[HBM] * 11,
        out_specs=[VM] * 2 + [HBM],
        scratch_shapes=[pltpu.VMEM(x.shape, x.dtype) for x in arrays]
        + [pltpu.SMEM(x.shape, x.dtype) for x in lengths]
        + [
            pltpu.VMEM(out_weight.shape, out_weight.dtype),
            pltpu.SemaphoreType.DMA((11,)),
            pltpu.SemaphoreType.DMA((nf // FB,)),
            pltpu.VMEM((nf, joint), F32),
            pltpu.VMEM((nt, joint), F32),
            pltpu.VMEM((nf, joint), F32),
            pltpu.VMEM((nt, joint), F32),
            pltpu.VMEM((nf, nt), F32),
            pltpu.VMEM((nf, nt), F32),
            pltpu.VMEM((nt, 128), jnp.int32),
            pltpu.VMEM((block, vocab), F32),
            pltpu.VMEM((cells, joint + vocab), BF16),
        ],
        compiler_params=pltpu.CompilerParams(vmem_limit_bytes=BIG),
        name="joint_cells",
    )(*arrays, *lengths, out_weight)

    sums = jnp.concatenate([term_keep, swap(term_send)], axis=1)
    sums, stash = lax.optimization_barrier((sums, stash))
    own = exchange(sums).sum(0)
    rows = vocab // 32
    ow_keep, ow_send, features = pl.pallas_call(
        wgrad_kernel,
        out_shape=[shape(joint // 8, rows, 128)] * 2 + [jax.ShapeDtypeStruct((2, joint, 2 * nt), BF16)],
        in_specs=[HBM] + [VM] * 2,
        out_specs=[VM] * 3,
        scratch_shapes=[
            pltpu.VMEM((cells, joint + vocab), BF16),
            pltpu.VMEM((joint, vocab), F32),
            pltpu.SemaphoreType.DMA((4,)),
        ],
        compiler_params=pltpu.CompilerParams(vmem_limit_bytes=54 * 1024 * 1024),
        cost_estimate=pl.CostEstimate(
            flops=2 * cells * joint * vocab, bytes_accessed=3 * cells * vocab, transcendentals=0
        ),
        name="out_weight_grad",
    )(stash, gathered, partner)
    own, ow_send = lax.optimization_barrier((own, ow_send))
    partner_own = swap(own)
    payload = pl.pallas_call(
        pack_kernel,
        out_shape=jax.ShapeDtypeStruct((joint // 8, rows + 16, 128), jnp.int16),
        in_specs=[VM] * 5,
        out_specs=VM,
        scratch_shapes=[pltpu.VMEM((joint // 8, 8, 2 * width), F32)],
        compiler_params=pltpu.CompilerParams(vmem_limit_bytes=24 * 1024 * 1024),
        name="pack_shares",
    )(ow_keep, swap(ow_send), own, partner_own, features)
    shares = lax.all_to_all(payload, ("frame", "token"), 0, 0)
    own_rows = joint // 128
    enc_grad, pred_grad, enc_wgrad, pred_wgrad, out_wgrad, bias_grad = pl.pallas_call(
        last_kernel,
        out_shape=[
            shape(1, nf, width), shape(1, nt, width), shape(own_rows, joint), shape(own_rows, joint),
            shape(own_rows, vocab), shape(1, own_rows),
        ],
        in_specs=[VM] * 3,
        out_specs=[VM] * 6,
        compiler_params=pltpu.CompilerParams(vmem_limit_bytes=24 * 1024 * 1024),
        name="sum_shares",
    )(shares, own, partner_own)
    return enc_grad, pred_grad, enc_wgrad, pred_wgrad, out_wgrad, bias_grad[0]


def solution(mesh):
    in_specs = (
        P("batch", "frame", "token"),
        P("batch", "token", "frame"),
        P(),
        P(),
        P(),
        P(),
        P("batch", "frame", "token"),
        P("batch", "frame", "token"),
        P(),
        P(),
        P(None, "token"),
    )
    out_specs = (
        P("batch", "frame", "token"),
        P("batch", "token", "frame"),
        P(ALL, None),
        P(ALL, None),
        P(ALL, None),
        P(ALL),
    )
    return jax.shard_map(local, mesh=mesh, in_specs=in_specs, out_specs=out_specs, check_vma=False)
```

time: 410 us -> 87.5 us (0.21)
  blocking collectives: 131 us -> 38.8 us
  waiting for transfers between devices: 86.6 us -> 6.64 us
  other arithmetic: 70.7 us -> 2.63 us
  matrix products: 52.8 us -> 0 us
  local copies, waits for them, and re-layouts: 43.1 us -> 2.85 us
  Pallas kernels: 0 us -> 28.6 us
  between operations: 16.3 us -> 0.68 us
  starting transfers between devices: 0.12 us -> 6.58 us
  loops' own time: 6.18 us -> 0 us
    unnamed x6 -> x0, waiting for transfers between devices: 86.6 us -> none
    unnamed x1 -> x0, blocking collectives: 76.8 us -> none
    all_gather x2 -> x0, blocking collectives: 53.9 us -> none  [the longest x1 31 us: local(): pred_full = lax.all_gather(predictor_out, 'frame', axis=2, tiled=True)[0]]
    dot_general x30 -> x0, matrix products: 52.8 us -> none  [the longest x8 16.3 us: work_block(): logits = jnp.dot(hidden, out_weight, preferred_element_type=jnp.float32)]
    all_to_all x0 -> x2, blocking collectives: none -> 38.8 us  [the longest x1 24.2 us: local(): shares = lax.all_to_all(payload, ('frame', 'token'), 0, 0)]
    add x32 -> x0, other arithmetic: 32.5 us -> none  [the longest x8 26 us: row_step(): grad_out + block_terms[0]]
    pallas_call x0 -> x4, Pallas kernels: none -> 28.6 us  [the longest x1 16.7 us: local(): pl.pallas_call(cells_kernel, out_shape=[shape(n, nf, 2 * width), shape(n,...]
    convert_element_type x16 -> x0, other arithmetic: 14.2 us -> none  [the longest x8 7.52 us: logit_grad(): return grad.astype(jnp.bfloat16)]
  transfers between devices with their start and end apart: 3 -> 6, of which waited for: 2 -> 6; matrix products, arithmetic and copies ran while one was open for 3% -> 0% of each run, Pallas kernels for 0% -> 11%
where the time goes in v1:
time: 87.5 us; the launch traced here: 86.7 us
  blocking collectives  38.8 us (44%)
  Pallas kernels  28.6 us (33%)
  waiting for transfers between devices  6.64 us (8%)
  starting transfers between devices  6.58 us (8%)
  local copies, waits for them, and re-layouts  2.85 us (3%)
  other arithmetic  2.63 us (3%)
    all_to_all x1, blocking collectives, local(): shares = lax.all_to_all(payload, ('frame', 'token'), 0, 0)  24.2 us
    pallas_call x1, Pallas kernels, local(): pl.pallas_call(cells_kernel, out_shape=[shape(n, nf, 2 * width), shape(n,...  16.7 us
    all_to_all x1, blocking collectives, exchange(): return lax.all_to_all(x, ALL, 0, 0, axis_index_groups=groups)  14.6 us
    pallas_call x1, Pallas kernels, local(): pl.pallas_call(wgrad_kernel, out_shape=[shape(joint // 8, rows, 128)] * 2...  9.94 us
    ppermute x5, waiting for transfers between devices, swap(): return lax.ppermute(x, 'batch', [(0, 1), (1, 0)])  6.15 us
    all_to_all x1, starting transfers between devices, exchange(): return lax.all_to_all(x, ALL, 0, 0, axis_index_groups=groups)  4.35 us
    unnamed x8, local copies, waits for them, and re-layouts  2.83 us
    ppermute x5, starting transfers between devices, swap(): return lax.ppermute(x, 'batch', [(0, 1), (1, 0)])  2.24 us
  transfers between devices with their start and end apart: 6, of which 6 were waited for; matrix products, arithmetic and copies ran while one was open for 0% of the time, Pallas kernels for 11%

profile of v1, /device:TPU:1, one launch (start us, length us, event | category | flops | bytes accessed | tf_op | source)
XLA Modules:
  0.0 86.7 jit_solution(7824469120735126699)
XLA Ops:
  0.6 0.7 select_bitcast_fusion.1
  1.4 1.4 %collective-permute-start = (bf16[64,64]{1,0:T(8,128)(2,1)S(1)}, bf16[64,64]{1,0:T(8,128)(2,1)S(1)}, u32[]{:S(2)}, u32[]{:S(2)}) collective-permute-start(bf16[64,64]{1,0:T(8,128)(2,1)S(1)} %get-tuple-element.39), channel_id=1, source_target_pairs={{0,1},{1,0},{2,3},{3,2},{4,5},{5,4},{6,7},{7,6},{8,9},{9,8},{10,11... | collective-permute-start | bytes 24584 | tf_op jit(solution)/shard_map/ppermute | solution.py:278
  2.8 0.8 collective-permute-done
  3.6 0.1 pad_maximum_fusion.1
  3.7 14.6 %all_to_all.15.g_hbm.g_ref = bf16[8,64,128]{2,1,0:T(8,128)(2,1)S(1)} all-to-all(bf16[8,64,128]{2,1,0:T(8,128)(2,1)S(1)} %broadcast_in_dim.4), channel_id=1, replica_groups={{0,2,4,6,8,10,12,14},{16,18,20,22,24,26,28,30},{32,34,36,38,40,42,44,46..., dimensions={0} | all-to-all | bytes 262144 | tf_op jit(solution)/shard_map/all_to_all | solution.py:281
  18.4 0.0 copy-start.2
  18.4 0.0 collective-permute-start.1
  18.4 1.3 %collective-permute-done.1.h_hbm.h_ref = bf16[8,64,128]{2,1,0:T(8,128)(2,1)S(1)} collective-permute-done((bf16[8,64,128]{2,1,0:T(8,128)(2,1)S(1)}, bf16[8,64,128]{2,1,0:T(8,128)(2,1)S(1)}, u32[]{:S(2)}, u32[]{:S(2)}) %collective-permute-start.1) | collective-permute-done | bytes 131104 | tf_op jit(solution)/shard_map/ppermute | solution.py:278
  19.7 0.0 copy-start.3
  19.7 0.0 copy-done.2
  19.7 0.6 copy-done.3
  20.4 16.7 %joint_cells.1 = (f32[8,64,128]{2,1,0:T(8,128)}, f32[8,64,128]{2,1,0:T(8,128)}, bf16[4096,1536]{1,0:T(8,128)(2,1)}) custom-call(bf16[8,64,128]{2,1,0:T(8,128)(2,1)} %copy-done.2, bf16[8,64,128]{2,1,0:T(8,128)(2,1)} %copy-done.3, bf16[512,512]{1,0:T(8,128)(2,1)} %encw_hbm.1, bf16[512,512]{1,0:T(8,128)(2,1)} %predw_hbm.1, f32[1,512]{1,0:T(1,128)} %bitcast.6, ...), custom_call_target="tpu_custom_call" | custom-call | tf_op jit(solution)/shard_map/joint_cells/pallas_call | solution.py:294
  37.0 0.2 collective-permute-start.2
  37.3 1.6 %collective-permute-done.2 = f32[8,64,128]{2,1,0:T(8,128)S(1)} collective-permute-done((f32[8,64,128]{2,1,0:T(8,128)}, f32[8,64,128]{2,1,0:T(8,128)S(1)}, u32[]{:S(2)}, u32[]{:S(2)}) %collective-permute-start.2) | collective-permute-done | bytes 262176 | tf_op jit(solution)/shard_map/ppermute | solution.py:278
  38.9 1.8 %pad_maximum_fusion = f32[8,128,128]{2,1,0:T(8,128)} fusion(f32[8,64,128]{2,1,0:T(8,128)S(1)} %collective-permute-done.2, f32[8,64,128]{2,1,0:T(8,128)} %get-tuple-element.22), kind=kLoop, calls=%fused_computation | loop fusion | flops 131072 | bytes 1048576 | tf_op jit(solution)/shard_map/concatenate | solution.py:321
  40.6 4.3 %all-to-all-start.1 = ((f32[8,128,128]{2,1,0:T(8,128)}), f32[8,128,128]{2,1,0:T(8,128)S(1)}, u32[]{:S(2)}, u32[]{:S(2)}) async-start(f32[8,128,128]{2,1,0:T(8,128)} %pad_maximum_fusion), calls=%async_computation.1 | async-start | bytes 1048576 | tf_op jit(solution)/shard_map/all_to_all | solution.py:281
  45.0 9.9 %out_weight_grad.1 = (f32[64,32,128]{2,1,0:T(8,128)}, f32[64,32,128]{2,1,0:T(8,128)}, bf16[2,512,128]{2,1,0:T(8,128)(2,1)}) custom-call(bf16[4096,1536]{1,0:T(8,128)(2,1)} %get-tuple-element.25.stash_hbm, bf16[8,64,128]{2,1,0:T(8,128)(2,1)} %copy-done.2, bf16[8,64,128]{2,1,0:T(8,128)(2,1)} %copy-done.3), custom_call_target="tpu_custom_call" | custom-call | flops 4294967296 | bytes 12582912 | tf_op jit(solution)/shard_map/out_weight_grad/pallas_call | solution.py:325
  54.9 0.5 all-to-all-done.1
  55.5 0.3 collective-permute-start.3
  55.7 0.3 collective-permute-start.4
  56.0 2.2 %collective-permute-done.4.partner_ref = f32[128,128]{1,0:T(8,128)S(1)} collective-permute-done((f32[128,128]{1,0:T(8,128)S(1)}, f32[128,128]{1,0:T(8,128)S(1)}, u32[]{:S(2)}, u32[]{:S(2)}) %collective-permute-start.4) | collective-permute-done | bytes 65568 | tf_op jit(solution)/shard_map/ppermute | solution.py:278
  58.3 0.1 collective-permute-done.3.recv_ref
  58.4 0.0 copy-start
  58.4 1.2 %copy-done = f32[64,32,128]{2,1,0:T(8,128)S(1)} copy-done((f32[64,32,128]{2,1,0:T(8,128)S(1)}, f32[64,32,128]{2,1,0:T(8,128)}, u32[]{:S(2)}) %copy-start) | copy-done | bytes 1048600
  59.6 0.0 copy-start.1
  59.6 0.9 %copy-done.1 = bf16[2,512,128]{2,1,0:T(8,128)(2,1)S(1)} copy-done((bf16[2,512,128]{2,1,0:T(8,128)(2,1)S(1)}, bf16[2,512,128]{2,1,0:T(8,128)(2,1)}, u32[]{:S(2)}) %copy-start.1) | copy-done | bytes 262168
  60.6 0.9 %pack_shares.1 = s16[64,48,128]{2,1,0:T(8,128)(2,1)S(1)} custom-call(f32[64,32,128]{2,1,0:T(8,128)S(1)} %copy-done, f32[64,32,128]{2,1,0:T(8,128)S(1)} %collective-permute-done.3.recv_ref, f32[128,128]{1,0:T(8,128)S(1)} %reduce_sum.9.own_ref, f32[128,128]{1,0:T(8,128)S(1)} %collective-permute-done.4.partner_ref, bf16[2,512,128]{2,1,0:T(8,128)(2,1)S(1)} %copy-done.1), custom_call_target="tpu_custom_call" | custom-call | tf_op jit(solution)/shard_map/pack_shares/pallas_call | solution.py:343
  61.5 24.2 %all_to_all.16.z_ref = s16[64,48,128]{2,1,0:T(8,128)(2,1)S(1)} all-to-all(s16[64,48,128]{2,1,0:T(8,128)(2,1)S(1)} %pack_shares.1), channel_id=1, replica_groups=mesh['frame'=8,'token'=8,'batch'=2] {'frame','token'}, dimensions={0} | all-to-all | bytes 1572864 | tf_op jit(solution)/shard_map/all_to_all | solution.py:352
  85.7 1.0 %sum_shares.1 = (f32[1,64,64]{2,1,0:T(8,128)}, f32[1,64,64]{2,1,0:T(8,128)}, f32[4,512]{1,0:T(4,128)}, f32[4,512]{1,0:T(4,128)}, f32[4,1024]{1,0:T(4,128)}, /*index=5*/f32[1,4]{1,0:T(1,128)}) custom-call(s16[64,48,128]{2,1,0:T(8,128)(2,1)S(1)} %all_to_all.16.z_ref, f32[128,128]{1,0:T(8,128)S(1)} %reduce_sum.9.own_ref, ...), custom_call_target="tpu_custom_call" | custom-call | tf_op jit(solution)/shard_map/sum_shares/pallas_call | solution.py:354
  (2 shorter events, 0.1 us)
Async XLA Ops:
  1.4 2.3 %collective-permute-start = (bf16[64,64]{1,0:T(8,128)(2,1)S(1)}, bf16[64,64]{1,0:T(8,128)(2,1)S(1)}, u32[]{:S(2)}, u32[]{:S(2)}) collective-permute-start(bf16[64,64]{1,0:T(8,128)(2,1)S(1)} %get-tuple-element.39), channel_id=1, source_target_pairs={{0,1},{1,0},{2,3},{3,2},{4,5},{5,4},{6,7},{7,6},{8,9},{9,8},{10,11... | collective-permute-start | bytes 24584 | tf_op jit(solution)/shard_map/ppermute | solution.py:278
  18.4 1.4 %copy-start.2 = (bf16[8,64,128]{2,1,0:T(8,128)(2,1)}, bf16[8,64,128]{2,1,0:T(8,128)(2,1)S(1)}, u32[]{:S(2)}) copy-start(bf16[8,64,128]{2,1,0:T(8,128)(2,1)S(1)} %all_to_all.15.g_hbm.g_ref) | copy-start | bytes 393220
  18.4 1.3 %collective-permute-start.1 = (bf16[8,64,128]{2,1,0:T(8,128)(2,1)S(1)}, bf16[8,64,128]{2,1,0:T(8,128)(2,1)S(1)}, u32[]{:S(2)}, u32[]{:S(2)}) collective-permute-start(bf16[8,64,128]{2,1,0:T(8,128)(2,1)S(1)} %all_to_all.15.g_hbm.g_ref), channel_id=1, source_target_pairs={{0,1},{1,0},{2,3},{3,2},{4,5},{5,4},{6,7},{7,6},{8,9},{9,8},{10,11... | collective-permute-start | bytes 393224 | tf_op jit(solution)/shard_map/ppermute | solution.py:278
  19.7 0.7 copy-start.3
  37.0 1.8 %collective-permute-start.2 = (f32[8,64,128]{2,1,0:T(8,128)}, f32[8,64,128]{2,1,0:T(8,128)S(1)}, u32[]{:S(2)}, u32[]{:S(2)}) collective-permute-start(f32[8,64,128]{2,1,0:T(8,128)} %get-tuple-element.23), channel_id=1, source_target_pairs={{0,1},{1,0},{2,3},{3,2},{4,5},{5,4},{6,7},{7,6},{8,9},{9,8},{10,11... | collective-permute-start | bytes 786440 | tf_op jit(solution)/shard_map/ppermute | solution.py:278
  40.6 14.8 %all-to-all-start.1 = ((f32[8,128,128]{2,1,0:T(8,128)}), f32[8,128,128]{2,1,0:T(8,128)S(1)}, u32[]{:S(2)}, u32[]{:S(2)}) async-start(f32[8,128,128]{2,1,0:T(8,128)} %pad_maximum_fusion), calls=%async_computation.1 | async-start | bytes 1048576 | tf_op jit(solution)/shard_map/all_to_all | solution.py:281
  55.5 3.0 %collective-permute-start.3 = (f32[64,32,128]{2,1,0:T(8,128)}, f32[64,32,128]{2,1,0:T(8,128)S(1)}, u32[]{:S(2)}, u32[]{:S(2)}) collective-permute-start(f32[64,32,128]{2,1,0:T(8,128)} %get-tuple-element.29), channel_id=1, source_target_pairs={{0,1},{1,0},{2,3},{3,2},{4,5},{5,4},{6,7},{7,6},{8,9},{9,8},{10,11... | collective-permute-start | bytes 3145736 | tf_op jit(solution)/shard_map/ppermute | solution.py:278
  55.7 2.6 %collective-permute-start.4 = (f32[128,128]{1,0:T(8,128)S(1)}, f32[128,128]{1,0:T(8,128)S(1)}, u32[]{:S(2)}, u32[]{:S(2)}) collective-permute-start(f32[128,128]{1,0:T(8,128)S(1)} %reduce_sum.9.own_ref), channel_id=1, source_target_pairs={{0,1},{1,0},{2,3},{3,2},{4,5},{5,4},{6,7},{7,6},{8,9},{9,8},{10,11... | collective-permute-start | bytes 196616 | tf_op jit(solution)/shard_map/ppermute | solution.py:278
  58.4 1.2 %copy-start = (f32[64,32,128]{2,1,0:T(8,128)S(1)}, f32[64,32,128]{2,1,0:T(8,128)}, u32[]{:S(2)}) copy-start(f32[64,32,128]{2,1,0:T(8,128)} %get-tuple-element.26.keep_ref) | copy-start | bytes 3145732
  59.6 0.9 %copy-start.1 = (bf16[2,512,128]{2,1,0:T(8,128)(2,1)S(1)}, bf16[2,512,128]{2,1,0:T(8,128)(2,1)}, u32[]{:S(2)}) copy-start(bf16[2,512,128]{2,1,0:T(8,128)(2,1)} %get-tuple-element.31.feat_ref) | copy-start | bytes 786436
